TPU v7x, 128 devices: a whole 4x4x4 slice. The times are simulated.
128 devices in a mesh: rep: 4 (over z), ten: 32 (over x, y, core).
Axes of the slice: x: 4, y: 4, z: 4, core: 2. Of those that a mesh axis runs over, the one named last changes fastest.
Arguments:
- blocks: bfloat16 [64, 512, 4096], P(None, 'ten'), may hold values from -0.5 to 0.5
- col_counts: int32 [32], replicated, may hold values from 1 to 4, 64 in all
- block_sizes: int32 [32], replicated, may hold values from 32 to 64
- occ_coeff: bfloat16 [2048, 256], P(None, 'rep'), may hold values from -1.5 to 1.5
- occ_weight: float32 [256], P('rep'), may hold values from 0.1 to 1
- virt_green: bfloat16 [2048, 2048], replicated, may hold values from -0.125 to 0.125
Outputs:
- chi: float32 [512, 512], P('ten')
Inputs may be any that keep to these rules, and one draw needn't show every extreme that they name: `col_counts`: each block column holds 1 to 4 nonzero blocks, 64 in all, and some column holds exactly 4.
All inputs are finite; a program needn't handle non-finite values.
Results may differ from a plain program's by a relative error of at most 0.0047.
Values may be sent and summed in bfloat16 or wider, within the bound.
No kernel may reach another device: no remote copies, remote signals or barrier semaphores. Data moves between devices by JAX's collectives and lax.ppermute only.
A program may use at most 192 MiB of HBM per device.

v0:
```python
import functools

import jax
import jax.numpy as jnp
from jax import lax
from jax.experimental import pallas as pl
from jax.experimental.pallas import tpu as pltpu
from jax.sharding import PartitionSpec as P

BS = 64
MOST = 4
LANES = 128
MIB = 1024 * 1024
BUFFERS = 4
WIDTHS = (12, 13, 16)
FIRST = 4
LATER = 51


def prefix_sums(counts_ref, into):
    total = jnp.int32(0)
    for b in range(counts_ref.shape[0]):
        into[b] = total
        total = total + counts_ref[b]
    return total


def targets(position, sizes_ref, offsets, m):
    size0, size1 = sizes_ref[2 * m], sizes_ref[2 * m + 1]
    start = offsets[2 * m]
    second = position >= BS
    local = jnp.where(second, position - BS, position)
    place = (local + jnp.where(second, start + size0, start)) & (LANES - 1)
    return jnp.where(local < jnp.where(second, size1, size0), place, -1)


def half_kernel(lo, his, counts_ref, sizes_ref, occ_ref, blocks_ref, *refs):
    outs = refs[: len(his)]
    held, occ32, slots, turned, weights, carry, stage, starts, offsets, sems, out_sem = refs[len(his) :]
    block_count = counts_ref.shape[0]
    pair_count, aux_rows, _ = blocks_ref.shape
    occ_count = occ_ref.shape[1]
    half_x = BS // 2
    pitch = half_x + 1
    turned_pitch = aux_rows + 1
    window = 2 * MOST
    last_pair = block_count // 2

    prefix_sums(counts_ref, starts)
    used = prefix_sums(sizes_ref, offsets)
    hi = jnp.int32(his[-1])
    for smaller in reversed(his[:-1]):
        hi = jnp.where(used <= smaller * LANES, smaller, hi)

    def count_before(limit):
        return sum((offsets[2 * m] < limit).astype(jnp.int32) for m in range(last_pair))

    m_lo = jnp.int32(0) if lo == 0 else count_before(lo * LANES + 1) - 1
    m_hi = count_before(hi * LANES)

    def base_of(m):
        return jnp.minimum(starts[2 * m], pair_count - window)

    def fetch(m):
        slot = m & (BUFFERS - 1)
        return pltpu.make_async_copy(blocks_ref.at[pl.ds(base_of(m), window)], held.at[slot], sems.at[slot])

    for ahead in range(BUFFERS - 1):

        @pl.when(m_lo + ahead < m_hi)
        def _(ahead=ahead):
            fetch(m_lo + ahead).start()

    occ32[...] = occ_ref[...].astype(jnp.float32)
    slots[...] = jnp.zeros_like(slots)
    carry[...] = jnp.zeros_like(carry)
    turned[...] = jnp.zeros_like(turned)

    twice = 2 * lax.broadcasted_iota(jnp.int32, (half_x, occ_count), 0)
    low = lax.broadcasted_iota(jnp.int32, (BS, LANES), 1) < BS
    square_row = lax.broadcasted_iota(jnp.int32, (LANES, LANES), 0)
    square_lane = lax.broadcasted_iota(jnp.int32, (LANES, LANES), 1)

    def set_weights(m):
        for side in range(2):
            b = 2 * m + side
            count = counts_ref[b]
            rows = [[], []]
            for j in range(MOST):
                row = b + ((j + 1) // 2 if j % 2 == 1 else -(j // 2))
                row = jnp.where(row < 0, row + block_count, row)
                row = jnp.where(row >= block_count, row - block_count, row)
                size = jnp.where(j < count, sizes_ref[row], 0)
                for parity in range(2):
                    coeff = occ32[pl.ds(row * BS + parity, half_x, stride=2), :]
                    rows[parity].append(jnp.where(twice + parity < size, coeff, 0.0))
            for parity in range(2):
                weights[side, parity * occ_count : (parity + 1) * occ_count, :] = jnp.transpose(
                    jnp.concatenate(rows[parity], axis=0)
                ).astype(jnp.bfloat16)

    def turn_blocks(m):
        slot = m & (BUFFERS - 1)
        base = base_of(m)
        for side in range(2):
            first, count = starts[2 * m + side] - base, counts_ref[2 * m + side]
            for j in range(MOST):

                @pl.when(j < count)
                def _(side=side, j=j, first=first):
                    for t in range(half_x):
                        piece = held[slot, first + j, :, t * LANES : (t + 1) * LANES]
                        slots[side, j, pl.ds(t, aux_rows, stride=pitch), :] = piece.astype(jnp.float32)

    def multiply():
        for pp in range(aux_rows // 2):
            sums = []
            for side in range(2):
                cols = [
                    jnp.concatenate(
                        [slots[side, j, p * pitch : p * pitch + half_x, :] for j in range(MOST)], axis=0
                    ).astype(jnp.bfloat16)
                    for p in (2 * pp, 2 * pp + 1)
                ]
                sums.append(
                    jnp.dot(weights[side], jnp.concatenate(cols, axis=1), preferred_element_type=jnp.float32)
                )
            for q in range(2):
                even0 = sums[0][:BS, q * LANES : (q + 1) * LANES]
                odd0 = sums[0][BS:, q * LANES : (q + 1) * LANES]
                even1 = sums[1][:BS, q * LANES : (q + 1) * LANES]
                odd1 = sums[1][BS:, q * LANES : (q + 1) * LANES]
                turned[pl.ds(2 * pp + q, occ_count, stride=turned_pitch), :] = jnp.where(
                    low, even0, odd1
                ) + pltpu.roll(jnp.where(low, even1, odd0), BS, 1)

    def pack(m, valid):
        start = offsets[2 * m]
        tile, split = start >> 7, start & (LANES - 1)
        filled = split + sizes_ref[2 * m] + sizes_ref[2 * m + 1]
        full = valid & (filled >= LANES)
        select = square_lane == jnp.where(valid, targets(square_row, sizes_ref, offsets, m), -1)
        select = select.astype(jnp.bfloat16)
        here = square_lane >= split
        column = pl.ds(pl.multiple_of(jnp.maximum(tile - lo, 0) * LANES, LANES), LANES)
        group = LANES // aux_rows
        for g in range(occ_count // group):
            values = jnp.concatenate(
                [turned[i * turned_pitch : i * turned_pitch + aux_rows, :] for i in range(g * group, (g + 1) * group)],
                axis=0,
            ).astype(jnp.bfloat16)
            moved = jnp.dot(values, select, preferred_element_type=jnp.float32)
            rows = slice(g * LANES, (g + 1) * LANES)
            current = carry[rows, :] + jnp.where(here, moved, 0.0)
            stage[rows, column] = current.astype(jnp.bfloat16)
            carry[rows, :] = jnp.where(full, jnp.where(here, 0.0, moved), current)
        return jnp.where(filled > LANES, tile + 1, -1)

    set_weights(m_lo)

    def column_pair(m, state):
        @pl.when(m + BUFFERS - 1 < m_hi)
        def _():
            fetch(m + BUFFERS - 1).start()

        fetch(m).wait()
        turn_blocks(m)
        pack(jnp.maximum(m - 1, m_lo), m > m_lo)
        multiply()
        set_weights(jnp.minimum(m + 1, last_pair - 1))
        return state

    lax.fori_loop(m_lo, m_hi, column_pair, 0)
    spill = pack(m_hi - 1, m_hi > m_lo)

    def zero(tile, state):
        stage[:, pl.ds(pl.multiple_of((tile - lo) * LANES, LANES), LANES)] = jnp.zeros(
            (stage.shape[0], LANES), jnp.bfloat16
        )
        return state

    lax.fori_loop(jnp.maximum((used + LANES - 1) >> 7, lo), hi, zero, 0)

    @pl.when((spill >= lo) & (spill < hi))
    def _():
        stage[:, pl.ds(pl.multiple_of((spill - lo) * LANES, LANES), LANES)] = carry[...].astype(jnp.bfloat16)

    for out_ref, tiles in zip(outs, his):

        @pl.when(hi == tiles)
        def _(out_ref=out_ref, tiles=tiles):
            copy = pltpu.make_async_copy(stage.at[:, : (tiles - lo) * LANES], out_ref, out_sem)
            copy.start()
            copy.wait()


def half_transform(blocks, col_counts, block_sizes, occ, lo, his):
    pair_count, aux_rows, flat = blocks.shape
    block_count = col_counts.shape[0]
    occ_count = occ.shape[1]
    smem = pl.BlockSpec(memory_space=pltpu.SMEM)
    vmem = pl.BlockSpec(memory_space=pltpu.VMEM)
    hbm = pl.BlockSpec(memory_space=pltpu.HBM)
    return pl.pallas_call(
        functools.partial(half_kernel, lo, his),
        out_shape=[jax.ShapeDtypeStruct((occ_count * aux_rows, (hi - lo) * LANES), jnp.bfloat16) for hi in his],
        in_specs=[smem, smem, vmem, hbm],
        out_specs=[hbm] * len(his),
        scratch_shapes=[
            pltpu.VMEM((BUFFERS, 2 * MOST, aux_rows, flat), jnp.bfloat16),
            pltpu.VMEM(occ.shape, jnp.float32),
            pltpu.VMEM((2, MOST, aux_rows * (BS // 2 + 1), LANES), jnp.float32),
            pltpu.VMEM((occ_count * (aux_rows + 1), LANES), jnp.float32),
            pltpu.VMEM((2, 2 * occ_count, MOST * BS // 2), jnp.bfloat16),
            pltpu.VMEM((occ_count * aux_rows, LANES), jnp.float32),
            pltpu.VMEM((occ_count * aux_rows, (his[-1] - lo) * LANES), jnp.bfloat16),
            pltpu.SMEM((block_count,), jnp.int32),
            pltpu.SMEM((block_count,), jnp.int32),
            pltpu.SemaphoreType.DMA((BUFFERS,)),
            pltpu.SemaphoreType.DMA,
        ],
        compiler_params=pltpu.CompilerParams(vmem_limit_bytes=60 * MIB),
        cost_estimate=pl.CostEstimate(flops=8 * 10**9, bytes_accessed=8 * MIB, transcendentals=0),
        name="half_transform",
    )(col_counts, block_sizes, occ, blocks)


def pack_kernel(sizes_ref, green_ref, out_ref, packed_rows, row_carry, lane_carry, offsets):
    basis_count = green_ref.shape[0]
    width = out_ref.shape[0]
    last_pair = sizes_ref.shape[0] // 2
    used = prefix_sums(sizes_ref, offsets)
    tiles = (used + LANES - 1) >> 7
    square_row = lax.broadcasted_iota(jnp.int32, (LANES, LANES), 0)
    square_lane = lax.broadcasted_iota(jnp.int32, (LANES, LANES), 1)
    strip = 4 * LANES
    row_carry[...] = jnp.zeros_like(row_carry)
    lane_carry[...] = jnp.zeros_like(lane_carry)

    def place(m):
        start = offsets[2 * m]
        split = start & (LANES - 1)
        return start >> 7, split, split + sizes_ref[2 * m] + sizes_ref[2 * m + 1]

    def at(tile):
        return pl.ds(pl.multiple_of(tile * LANES, LANES), LANES)

    def pack_rows(m, state):
        tile, split, filled = place(m)
        select = (square_row == targets(square_lane, sizes_ref, offsets, m)).astype(jnp.bfloat16)
        here = lax.broadcasted_iota(jnp.int32, (LANES, strip), 0) >= split
        for s in range(basis_count // strip):
            lanes = slice(s * strip, (s + 1) * strip)
            moved = jnp.dot(select, green_ref[at(m), lanes], preferred_element_type=jnp.float32)
            current = row_carry[:, lanes] + jnp.where(here, moved, 0.0)
            packed_rows[at(tile), lanes] = current.astype(jnp.bfloat16)
            row_carry[:, lanes] = jnp.where(filled >= LANES, jnp.where(here, 0.0, moved), current)
        return jnp.where(filled > LANES, tile + 1, -1)

    spill = lax.fori_loop(0, last_pair, pack_rows, jnp.int32(-1))

    def zero_rows(tile, state):
        packed_rows[at(tile), :] = jnp.zeros((LANES, basis_count), jnp.bfloat16)
        return state

    lax.fori_loop(tiles, width // LANES, zero_rows, 0)

    @pl.when(spill >= 0)
    def _():
        packed_rows[at(spill), :] = row_carry[...].astype(jnp.bfloat16)

    def pack_lanes(m, state):
        tile, split, filled = place(m)
        select = (square_lane == targets(square_row, sizes_ref, offsets, m)).astype(jnp.bfloat16)
        here = square_lane >= split
        for r in range(width // LANES):
            rows = slice(r * LANES, (r + 1) * LANES)
            moved = jnp.dot(packed_rows[rows, at(m)], select, preferred_element_type=jnp.float32)
            current = lane_carry[rows, :] + jnp.where(here, moved, 0.0)
            out_ref[rows, at(tile)] = current.astype(jnp.bfloat16)
            lane_carry[rows, :] = jnp.where(filled >= LANES, jnp.where(here, 0.0, moved), current)
        return state

    lax.fori_loop(0, last_pair, pack_lanes, 0)

    def zero_lanes(tile, state):
        out_ref[:, at(tile)] = jnp.zeros((width, LANES), jnp.bfloat16)
        return state

    lax.fori_loop(tiles, width // LANES, zero_lanes, 0)

    @pl.when(spill >= 0)
    def _():
        out_ref[:, at(spill)] = lane_carry[...].astype(jnp.bfloat16)


def pack_green(block_sizes, virt_green, width):
    basis_count = virt_green.shape[0]
    vmem = pl.BlockSpec(memory_space=pltpu.VMEM)
    return pl.pallas_call(
        pack_kernel,
        out_shape=jax.ShapeDtypeStruct((width, width), jnp.bfloat16),
        in_specs=[pl.BlockSpec(memory_space=pltpu.SMEM), vmem],
        out_specs=vmem,
        scratch_shapes=[
            pltpu.VMEM((width, basis_count), jnp.bfloat16),
            pltpu.VMEM((LANES, basis_count), jnp.float32),
            pltpu.VMEM((width, LANES), jnp.float32),
            pltpu.SMEM((block_sizes.shape[0],), jnp.int32),
        ],
        compiler_params=pltpu.CompilerParams(vmem_limit_bytes=60 * MIB),
        cost_estimate=pl.CostEstimate(flops=10 * 10**9, bytes_accessed=14 * MIB, transcendentals=0),
        name="pack_green",
    )(block_sizes, virt_green)


def dress_kernel(half_ref, green_ref, out_ref):
    sources, own, aux_rows, depth = half_ref.shape
    rows = sources * aux_rows
    for ii in range(own):
        out_ref[ii] = jnp.dot(
            half_ref[:, ii].reshape(rows, depth), green_ref[...], preferred_element_type=jnp.float32
        )


def column_start(step, tile, width):
    return pl.multiple_of(jnp.minimum(step * tile, width - tile), LANES)


def dress(half, green, tile):
    sources, own, aux_rows, depth = half.shape
    rows = sources * aux_rows
    width = green.shape[1]
    steps = pl.cdiv(width, tile)
    return pl.pallas_call(
        dress_kernel,
        grid=(steps,),
        out_shape=jax.ShapeDtypeStruct((own, rows, steps * tile), jnp.float32),
        in_specs=[
            pl.BlockSpec((sources, own, aux_rows, depth), lambda n: (0, 0, 0, 0)),
            pl.BlockSpec((pl.Element(depth), pl.Element(tile)), lambda n: (0, column_start(n, tile, width))),
        ],
        out_specs=pl.BlockSpec((own, rows, tile), lambda n: (0, 0, n)),
        compiler_params=pltpu.CompilerParams(vmem_limit_bytes=60 * MIB),
        cost_estimate=pl.CostEstimate(
            flops=2 * own * rows * depth * width,
            bytes_accessed=2 * own * rows * depth + 2 * depth * width + 4 * own * rows * width,
            transcendentals=0,
        ),
        name="dress",
    )(half, green)


def response_kernel(split, width, weight_ref, half0_ref, half1_ref, green_ref, part_ref, chi_ref, total):
    step = pl.program_id(0)
    sources, own, aux_rows, depth = half1_ref.shape
    rows = sources * aux_rows
    tile = green_ref.shape[1]
    start = column_start(step, tile, width)
    fresh = lax.broadcasted_iota(jnp.int32, (rows, tile), 1) >= step * tile - start

    @pl.when(step == 0)
    def _():
        total[...] = jnp.zeros_like(total)

    def add(half_ref, first):
        columns = pl.ds(pl.multiple_of(start - first, LANES), tile)
        left, right = [], []
        for ii in range(own):
            dressed = part_ref[ii] + jnp.dot(
                half1_ref[:, ii].reshape(rows, depth), green_ref[...], preferred_element_type=jnp.float32
            )
            right.append(jnp.where(fresh, dressed * weight_ref[ii], 0.0).astype(jnp.bfloat16))
            left.append(half_ref[:, ii, :, columns].reshape(rows, tile))
        total[...] += lax.dot_general(
            jnp.concatenate(left, axis=1),
            jnp.concatenate(right, axis=1),
            (((1,), (1,)), ((), ())),
            preferred_element_type=jnp.float32,
        )

    @pl.when(step < split // tile)
    def _():
        add(half0_ref, 0)

    @pl.when(step >= split // tile)
    def _():
        add(half1_ref, split)

    @pl.when(step == pl.num_programs(0) - 1)
    def _():
        chi_ref[...] = total[...].astype(chi_ref.dtype)


def response(half0, half1, weight, part, green, tile):
    sources, own, aux_rows, depth0 = half0.shape
    depth1 = half1.shape[3]
    rows = sources * aux_rows
    width = depth0 + depth1
    whole = lambda n: (0, 0, 0, 0)
    return pl.pallas_call(
        functools.partial(response_kernel, depth0, width),
        grid=(pl.cdiv(width, tile),),
        out_shape=jax.ShapeDtypeStruct((rows, rows), jnp.bfloat16),
        in_specs=[
            pl.BlockSpec(memory_space=pltpu.SMEM),
            pl.BlockSpec((sources, own, aux_rows, depth0), whole),
            pl.BlockSpec((sources, own, aux_rows, depth1), whole),
            pl.BlockSpec((pl.Element(depth1), pl.Element(tile)), lambda n: (depth0, column_start(n, tile, width))),
            pl.BlockSpec((own, rows, tile), lambda n: (0, 0, n)),
        ],
        out_specs=pl.BlockSpec((rows, rows), lambda n: (0, 0)),
        scratch_shapes=[pltpu.VMEM((rows, rows), jnp.float32)],
        compiler_params=pltpu.CompilerParams(vmem_limit_bytes=LATER * MIB),
        name="response",
    )(weight, half0, half1, green, part)


def finish(tiles, got, halves, block_sizes, weight, virt_green):
    devices, own, aux_rows, _ = got.shape
    half = halves[WIDTHS.index(tiles)].reshape(devices, own, aux_rows, (tiles - FIRST) * LANES)
    rest = lax.all_to_all(half, "ten", split_axis=0, concat_axis=0, tiled=True)
    green = pack_green(block_sizes, virt_green, tiles * LANES)
    tile = 512 if tiles % 4 == 0 else 256
    part = dress(got, green, tile)
    terms = response(got, rest, weight, part, green, tile).reshape(devices, aux_rows, devices * aux_rows)
    terms = lax.all_to_all(terms, "ten", split_axis=0, concat_axis=0, tiled=True)
    share = jnp.sum(terms.astype(jnp.float32), axis=0)
    groups = lax.axis_size("rep")
    one, two, three = (
        lax.ppermute(share, "rep", [(z, (z + step) % groups) for z in range(groups)]) for step in (1, 2, 3)
    )
    return (share + two) + (one + three)


def per_device(blocks, col_counts, block_sizes, occ_coeff, occ_weight, virt_green):
    devices = lax.axis_size("ten")
    aux_rows = blocks.shape[1]
    own = occ_coeff.shape[1] // devices
    (half,) = half_transform(blocks, col_counts, block_sizes, occ_coeff, 0, (FIRST,))
    half = half.reshape(devices, own, aux_rows, FIRST * LANES)
    got = lax.all_to_all(half, "ten", split_axis=0, concat_axis=0, tiled=True)
    halves = half_transform(blocks, col_counts, block_sizes, occ_coeff, FIRST, WIDTHS)
    weight = lax.dynamic_slice(occ_weight, (lax.axis_index("ten") * own,), (own,))
    used = jnp.sum(block_sizes)
    case = sum((used > tiles * LANES).astype(jnp.int32) for tiles in WIDTHS[:-1])
    return lax.switch(
        case,
        [functools.partial(finish, tiles) for tiles in WIDTHS],
        got, halves, block_sizes, weight, virt_green,
    )


def solution(mesh):
    return jax.shard_map(
        per_device,
        mesh=mesh,
        in_specs=(P(None, "ten", None), P(), P(), P(None, "rep"), P("rep"), P()),
        out_specs=P("ten", None),
        check_vma=False,
    )
```

profile of v0, /device:TPU:1, one launch (start us, length us, event | category | flops | bytes accessed | tf_op | source)
XLA Modules:
  0.0 101.2 jit_solution(18405331115322259019)
XLA Ops:
  0.0 1.9 %copy.10.occ_ref = bf16[2048,64]{1,0:T(8,128)(2,1)} copy(bf16[2048,64]{0,1:T(8,128)(2,1)} %param.12) | data formatting | bytes 524288 | tf_op args[3]
  1.9 0.0 copy-start.2
  1.9 0.0 copy-start.1
  2.0 8.1 %half_transform.3 = bf16[1024,512]{1,0:T(8,128)(2,1)} custom-call(s32[32]{0:T(128)} %counts_ref.3, s32[32]{0:T(128)} %sizes_ref.3, bf16[2048,64]{1,0:T(8,128)(2,1)} %copy.10.occ_ref, bf16[64,16,4096]{2,1,0:T(8,128)(2,1)} %blocks_ref.3), custom_call_target="tpu_custom_call" | custom-call | flops 8000000000 | bytes 8388608 | tf_op jit(solution)/shard_map/half_transform/pallas_call | solution.py:204
  10.1 8.6 %all-to-all-start.6 = ((bf16[32,2,16,512]{3,2,1,0:T(8,128)(2,1)}), bf16[32,2,16,512]{3,2,1,0:T(8,128)(2,1)S(1)}, u32[]{:S(2)}, u32[]{:S(2)}) async-start(bf16[32,2,16,512]{3,2,1,0:T(8,128)(2,1)} %bitcast.13), calls=%async_computation.6 | async-start | bytes 2097152 | tf_op jit(solution)/shard_map/all_to_all | solution.py:442
  18.7 0.0 copy-done.2
  18.7 0.6 reduce_sum.36
  20.7 0.0 copy-done.1
  20.7 0.1 dynamic_slice.3
  20.7 12.6 %half_transform.2 = (bf16[1024,1024]{1,0:T(8,128)(2,1)}, bf16[1024,1152]{1,0:T(8,128)(2,1)}, bf16[1024,1536]{1,0:T(8,128)(2,1)}) custom-call(s32[32]{0:T(128)} %counts_ref.3, s32[32]{0:T(128)S(1)} %copy-done.2, bf16[2048,64]{1,0:T(8,128)(2,1)} %copy.10.occ_ref, bf16[64,16,4096]{2,1,0:T(8,128)(2,1)} %blocks_ref.3), custom_call_target="tpu_custom_call" | custom-call | flops 8000000000 | bytes 8388608 | tf_op jit(solution)/shard_map/half_transform/pallas_call | solution.py:204
  33.4 2.3 %all-to-all-done.6 = bf16[32,2,16,512]{3,2,1,0:T(8,128)(2,1)S(1)} async-done(((bf16[32,2,16,512]{3,2,1,0:T(8,128)(2,1)}), bf16[32,2,16,512]{3,2,1,0:T(8,128)(2,1)S(1)}, u32[]{:S(2)}, u32[]{:S(2)}) %all-to-all-start.6) | async-done | bytes 1048608 | tf_op jit(solution)/shard_map/all_to_all | solution.py:442
  35.6 65.0 %conditional.1 = (f32[16,512]{1,0:T(8,128)S(1)}) conditional(s32[]{:T(128)} %clamp.3, (bf16[1024,1024]{1,0:T(8,128)(2,1)}, s32[32]{0:T(128)S(1)}, bf16[2048,2048]{1,0:T(8,128)(2,1)}, bf16[32,2,16,512]{3,2,1,0:T(8,128)(2,1)S(1)}, f32[2]{0:T(128)S(1)}) %tuple.24, (bf16[1024,1152]{1,0:T(8,128)(2,1)}, s32[32]{0:T(128)S(1)}, ...), branch_computations={%region_1.0_spmd, %region_3.0_spmd, %region_5.0_spmd} | conditional | flops 12148024320 | bytes 37814432 | solution.py:447
  35.6 5.1 %all-to-all-start = ((bf16[32,2,16,1024]{3,2,1,0:T(8,128)(2,1)}), bf16[32,2,16,1024]{3,2,1,0:T(8,128)(2,1)S(1)}, u32[]{:S(2)}, u32[]{:S(2)}) async-start(bf16[32,2,16,1024]{3,2,1,0:T(8,128)(2,1)} %bitcast.12), calls=%async_computation | async-start | bytes 4194304 | tf_op jit(solution)/shard_map/cond/branch_0_fun/all_to_all | solution.py:422
  40.8 15.6 %pack_green.3.green_ref = bf16[1536,1536]{1,0:T(8,128)(2,1)} custom-call(s32[32]{0:T(128)S(1)} %get-tuple-element.42.sizes_ref, bf16[2048,2048]{1,0:T(8,128)(2,1)} %get-tuple-element.43.green_ref), custom_call_target="tpu_custom_call" | custom-call | flops 10000000000 | bytes 14680064 | tf_op jit(solution)/shard_map/cond/branch_0_fun/pack_green/pallas_call | solution.py:300
  56.3 5.4 %dress.3.part_ref = f32[2,512,1536]{2,1,0:T(8,128)} custom-call(bf16[32,2,16,512]{3,2,1,0:T(8,128)(2,1)S(1)} %get-tuple-element.40.half_ref.half0_ref, bf16[1536,1536]{1,0:T(8,128)(2,1)} %pack_green.3.green_ref), custom_call_target="tpu_custom_call" | custom-call | flops 1610612736 | bytes 8912896 | tf_op jit(solution)/shard_map/cond/branch_0_fun/dress/pallas_call | solution.py:335
  61.8 7.3 %all-to-all-done.half1_ref = bf16[32,2,16,1024]{3,2,1,0:T(8,128)(2,1)S(1)} async-done(((bf16[32,2,16,1024]{3,2,1,0:T(8,128)(2,1)}), bf16[32,2,16,1024]{3,2,1,0:T(8,128)(2,1)S(1)}, u32[]{:S(2)}, u32[]{:S(2)}) %all-to-all-start) | async-done | bytes 2097184 | tf_op jit(solution)/shard_map/cond/branch_0_fun/all_to_all | solution.py:422
  69.1 7.7 %response.3 = bf16[512,512]{1,0:T(8,128)(2,1)S(1)} custom-call(f32[2]{0:T(128)S(1)} %get-tuple-element.38.weight_ref, bf16[32,2,16,512]{3,2,1,0:T(8,128)(2,1)S(1)} %get-tuple-element.40.half_ref.half0_ref, bf16[32,2,16,1024]{3,2,1,0:T(8,128)(2,1)S(1)} %all-to-all-done.half1_ref, bf16[1536,1536]{1,0:T(8,128)(2,1)} %pack_green.3.green_ref, ...), custom_call_target="tpu_custom_call" | custom-call | tf_op jit(solution)/shard_map/cond/branch_0_fun/response/pallas_call | solution.py:401
  76.8 15.3 %all_to_all.29 = bf16[32,16,512]{2,1,0:T(8,128)(2,1)S(1)} all-to-all(bf16[32,16,512]{2,1,0:T(8,128)(2,1)S(1)} %bitcast.7), channel_id=1, replica_groups=mesh['rep'=4,'ten'=32] {'ten'}, dimensions={0} | all-to-all | bytes 1048576 | tf_op jit(solution)/shard_map/cond/branch_0_fun/all_to_all | solution.py:427
  92.1 0.1 convert_reduce_fusion
  92.1 3.8 %collective-permute-start.2 = (f32[16,512]{1,0:T(8,128)S(1)}, f32[16,512]{1,0:T(8,128)S(1)}, u32[]{:S(2)}, u32[]{:S(2)}) collective-permute-start(f32[16,512]{1,0:T(8,128)S(1)} %convert_reduce_fusion), channel_id=1, source_target_pairs={{0,96},{32,0},{64,32},{96,64},{1,97},{33,1},{65,33},{97,65},{2,98}... | collective-permute-start | bytes 98312 | tf_op jit(solution)/shard_map/cond/branch_0_fun/ppermute | solution.py:431
  95.9 0.0 collective-permute-start.1
  95.9 1.4 %collective-permute-start = (f32[16,512]{1,0:T(8,128)S(1)}, f32[16,512]{1,0:T(8,128)S(1)}, u32[]{:S(2)}, u32[]{:S(2)}) collective-permute-start(f32[16,512]{1,0:T(8,128)S(1)} %convert_reduce_fusion), channel_id=1, source_target_pairs={{0,64},{32,96},{64,0},{96,32},{1,65},{33,97},{65,1},{97,33},{2,66}... | collective-permute-start | bytes 98312 | tf_op jit(solution)/shard_map/cond/branch_0_fun/ppermute | solution.py:431
  97.4 0.0 collective-permute-done.2
  97.4 2.6 %collective-permute-done.1 = f32[16,512]{1,0:T(8,128)S(1)} collective-permute-done((f32[16,512]{1,0:T(8,128)S(1)}, f32[16,512]{1,0:T(8,128)S(1)}, u32[]{:S(2)}, u32[]{:S(2)}) %collective-permute-start.1) | collective-permute-done | bytes 32800 | tf_op jit(solution)/shard_map/cond/branch_0_fun/ppermute | solution.py:431
  99.9 0.4 collective-permute-done
  100.6 0.0 copy-start
  100.6 0.6 copy-done
  (1 shorter events, 0.0 us)
Async XLA Ops:
  1.9 16.8 %copy-start.2 = (s32[32]{0:T(128)S(1)}, s32[32]{0:T(128)}, u32[]{:S(2)}) copy-start(s32[32]{0:T(128)} %sizes_ref.3) | copy-start | bytes 388
  1.9 18.7 %copy-start.1 = (f32[64]{0:T(128)S(1)}, f32[64]{0:T(128)}, u32[]{:S(2)}) copy-start(f32[64]{0:T(128)} %param.13) | copy-start | bytes 772
  10.1 25.6 %all-to-all-start.6 = ((bf16[32,2,16,512]{3,2,1,0:T(8,128)(2,1)}), bf16[32,2,16,512]{3,2,1,0:T(8,128)(2,1)S(1)}, u32[]{:S(2)}, u32[]{:S(2)}) async-start(bf16[32,2,16,512]{3,2,1,0:T(8,128)(2,1)} %bitcast.13), calls=%async_computation.6 | async-start | bytes 2097152 | tf_op jit(solution)/shard_map/all_to_all | solution.py:442
  35.6 33.5 %all-to-all-start = ((bf16[32,2,16,1024]{3,2,1,0:T(8,128)(2,1)}), bf16[32,2,16,1024]{3,2,1,0:T(8,128)(2,1)S(1)}, u32[]{:S(2)}, u32[]{:S(2)}) async-start(bf16[32,2,16,1024]{3,2,1,0:T(8,128)(2,1)} %bitcast.12), calls=%async_computation | async-start | bytes 4194304 | tf_op jit(solution)/shard_map/cond/branch_0_fun/all_to_all | solution.py:422
  92.1 5.2 %collective-permute-start.2 = (f32[16,512]{1,0:T(8,128)S(1)}, f32[16,512]{1,0:T(8,128)S(1)}, u32[]{:S(2)}, u32[]{:S(2)}) collective-permute-start(f32[16,512]{1,0:T(8,128)S(1)} %convert_reduce_fusion), channel_id=1, source_target_pairs={{0,96},{32,0},{64,32},{96,64},{1,97},{33,1},{65,33},{97,65},{2,98}... | collective-permute-start | bytes 98312 | tf_op jit(solution)/shard_map/cond/branch_0_fun/ppermute | solution.py:431
  95.9 4.0 %collective-permute-start.1 = (f32[16,512]{1,0:T(8,128)S(1)}, f32[16,512]{1,0:T(8,128)S(1)}, u32[]{:S(2)}, u32[]{:S(2)}) collective-permute-start(f32[16,512]{1,0:T(8,128)S(1)} %convert_reduce_fusion), channel_id=1, source_target_pairs={{0,32},{32,64},{64,96},{96,0},{1,33},{33,65},{65,97},{97,1},{2,34}... | collective-permute-start | bytes 98312 | tf_op jit(solution)/shard_map/cond/branch_0_fun/ppermute | solution.py:431
  95.9 4.4 %collective-permute-start = (f32[16,512]{1,0:T(8,128)S(1)}, f32[16,512]{1,0:T(8,128)S(1)}, u32[]{:S(2)}, u32[]{:S(2)}) collective-permute-start(f32[16,512]{1,0:T(8,128)S(1)} %convert_reduce_fusion), channel_id=1, source_target_pairs={{0,64},{32,96},{64,0},{96,32},{1,65},{33,97},{65,1},{97,33},{2,66}... | collective-permute-start | bytes 98312 | tf_op jit(solution)/shard_map/cond/branch_0_fun/ppermute | solution.py:431
  100.6 0.6 copy-start
where the time goes:
time: 102 us; the launch traced here: 101 us
  Pallas kernels  49.4 us (48%)
  starting transfers between devices  19 us (19%)
  blocking collectives  15.3 us (15%)
  waiting for transfers between devices  12.5 us (12%)
  local copies, waits for them, and re-layouts  2.64 us (3%)
  between operations  1.37 us (1%)
    pallas_call x2, Pallas kernels, half_transform(): pl.pallas_call(functools.partial(half_kernel, lo, his), out_shape=[jax.Sh...  20.7 us
    pallas_call x1, Pallas kernels, pack_green(): pl.pallas_call(pack_kernel, out_shape=jax.ShapeDtypeStruct((width, width)...  15.6 us
    all_to_all x1, blocking collectives, finish(): lax.all_to_all(terms, 'ten', split_axis=0, concat_axis=0, tiled=True)  15.3 us
    all_to_all x1, starting transfers between devices, per_device(): got = lax.all_to_all(half, 'ten', split_axis=0, concat_axis=0, tiled=True)  8.63 us
    pallas_call x1, Pallas kernels, response(): pl.pallas_call(functools.partial(response_kernel, depth0, width), grid=(p...  7.71 us
    all_to_all x1, waiting for transfers between devices, finish(): rest = lax.all_to_all(half, 'ten', split_axis=0, concat_axis=0, tiled=True)  7.31 us
    pallas_call x1, Pallas kernels, dress(): pl.pallas_call(dress_kernel, grid=(steps,), out_shape=jax.ShapeDtypeStruc...  5.42 us
    ppermute x3, starting transfers between devices, finish(): lax.ppermute(share, 'rep', [(z, (z + step) % groups) for z in range(group...  5.22 us
  transfers between devices with their start and end apart: 5, of which 4 were waited for; matrix products, arithmetic and copies ran while one was open for 1% of the time, Pallas kernels for 33%

commit v1 on v0

--- a/solution.py
+++ b/solution.py
@@ -39,7 +39,7 @@
     held, occ32, slots, turned, weights, carry, stage, starts, offsets, sems, out_sem = refs[len(his) :]
     block_count = counts_ref.shape[0]
     pair_count, aux_rows, _ = blocks_ref.shape
-    occ_count = occ_ref.shape[1]
+    occ_count = occ_ref.shape[0]
     half_x = BS // 2
     pitch = half_x + 1
     turned_pitch = aux_rows + 1
@@ -71,7 +71,9 @@
         def _(ahead=ahead):
             fetch(m_lo + ahead).start()
 
-    occ32[...] = occ_ref[...].astype(jnp.float32)
+    for c in range(occ_ref.shape[1] // LANES):
+        columns = slice(c * LANES, (c + 1) * LANES)
+        occ32[columns, :] = jnp.transpose(occ_ref[:, columns].astype(jnp.float32))
     slots[...] = jnp.zeros_like(slots)
     carry[...] = jnp.zeros_like(carry)
     turned[...] = jnp.zeros_like(turned)
@@ -222,7 +224,7 @@
         compiler_params=pltpu.CompilerParams(vmem_limit_bytes=60 * MIB),
         cost_estimate=pl.CostEstimate(flops=8 * 10**9, bytes_accessed=8 * MIB, transcendentals=0),
         name="half_transform",
-    )(col_counts, block_sizes, occ, blocks)
+    )(col_counts, block_sizes, occ.T, blocks)
 
 
 def pack_kernel(sizes_ref, green_ref, out_ref, packed_rows, row_carry, lane_carry, offsets):

time: 102 us -> 106 us (1.039)
  Pallas kernels: 49.4 us -> 55.2 us
  local copies, waits for them, and re-layouts: 2.64 us -> 0.69 us
    pallas_call x1, Pallas kernels: 7.71 us -> 10.9 us  [response(): pl.pallas_call(functools.partial(response_kernel, depth0, width), grid=(p...]
    pallas_call x1, Pallas kernels: 5.42 us -> 7.37 us  [dress(): pl.pallas_call(dress_kernel, grid=(steps,), out_shape=jax.ShapeDtypeStruc...]
    unnamed x7 -> x6, local copies, waits for them, and re-layouts: 2.56 us -> 0.62 us
  transfers between devices with their start and end apart: 5 -> 5, of which waited for: 4 -> 4; matrix products, arithmetic and copies ran while one was open for 1% -> 1% of each run, Pallas kernels for 33% -> 34%
where the time goes in v1:
time: 106 us
  Pallas kernels  55.2 us (52%)
  starting transfers between devices  18.9 us (18%)
  blocking collectives  15.3 us (14%)
  waiting for transfers between devices  13 us (12%)
  between operations  1.37 us (1%)
    pallas_call x2, Pallas kernels, half_transform(): pl.pallas_call(functools.partial(half_kernel, lo, his), out_shape=[jax.Sh...  20.8 us
    pallas_call x1, Pallas kernels, pack_green(): pl.pallas_call(pack_kernel, out_shape=jax.ShapeDtypeStruct((width, width)...  16.1 us
    all_to_all x1, blocking collectives, finish(): lax.all_to_all(terms, 'ten', split_axis=0, concat_axis=0, tiled=True)  15.3 us
    pallas_call x1, Pallas kernels, response(): pl.pallas_call(functools.partial(response_kernel, depth0, width), grid=(p...  10.9 us
    all_to_all x1, starting transfers between devices, per_device(): got = lax.all_to_all(half, 'ten', split_axis=0, concat_axis=0, tiled=True)  8.62 us
    all_to_all x1, waiting for transfers between devices, finish(): rest = lax.all_to_all(half, 'ten', split_axis=0, concat_axis=0, tiled=True)  7.65 us
    pallas_call x1, Pallas kernels, dress(): pl.pallas_call(dress_kernel, grid=(steps,), out_shape=jax.ShapeDtypeStruc...  7.37 us
    all_to_all x1, starting transfers between devices, finish(): rest = lax.all_to_all(half, 'ten', split_axis=0, concat_axis=0, tiled=True)  5.14 us
  transfers between devices with their start and end apart: 5, of which 4 were waited for; matrix products, arithmetic and copies ran while one was open for 1% of the time, Pallas kernels for 34%

profile of v1, /device:TPU:1, one launch (start us, length us, event | category | flops | bytes accessed | tf_op | source)
XLA Modules:
  0.0 105.6 jit_solution(12204900122614155828)
XLA Ops:
  0.0 0.0 copy-start.2
  0.0 0.0 copy-start.1
  0.0 8.2 %half_transform.3 = bf16[1024,512]{1,0:T(8,128)(2,1)} custom-call(s32[32]{0:T(128)} %counts_ref.3, s32[32]{0:T(128)} %sizes_ref.3, bf16[64,2048]{1,0:T(8,128)(2,1)} %bitcast.15, bf16[64,16,4096]{2,1,0:T(8,128)(2,1)} %blocks_ref.3), custom_call_target="tpu_custom_call" | custom-call | flops 8000000000 | bytes 8388608 | tf_op jit(solution)/shard_map/half_transform/pallas_call | solution.py:206
  8.2 8.6 %all-to-all-start.6 = ((bf16[32,2,16,512]{3,2,1,0:T(8,128)(2,1)}), bf16[32,2,16,512]{3,2,1,0:T(8,128)(2,1)S(1)}, u32[]{:S(2)}, u32[]{:S(2)}) async-start(bf16[32,2,16,512]{3,2,1,0:T(8,128)(2,1)} %bitcast.14), calls=%async_computation.6 | async-start | bytes 2097152 | tf_op jit(solution)/shard_map/all_to_all | solution.py:444
  16.9 0.0 copy-done.2
  16.9 0.6 reduce_sum.36
  18.8 0.0 copy-done.1
  18.8 0.1 dynamic_slice.3
  18.9 12.6 %half_transform.2 = (bf16[1024,1024]{1,0:T(8,128)(2,1)}, bf16[1024,1152]{1,0:T(8,128)(2,1)}, bf16[1024,1536]{1,0:T(8,128)(2,1)}) custom-call(s32[32]{0:T(128)} %counts_ref.3, s32[32]{0:T(128)S(1)} %copy-done.2, bf16[64,2048]{1,0:T(8,128)(2,1)} %bitcast.16, bf16[64,16,4096]{2,1,0:T(8,128)(2,1)} %blocks_ref.3), custom_call_target="tpu_custom_call" | custom-call | flops 8000000000 | bytes 8388608 | tf_op jit(solution)/shard_map/half_transform/pallas_call | solution.py:206
  31.5 2.3 %all-to-all-done.6 = bf16[32,2,16,512]{3,2,1,0:T(8,128)(2,1)S(1)} async-done(((bf16[32,2,16,512]{3,2,1,0:T(8,128)(2,1)}), bf16[32,2,16,512]{3,2,1,0:T(8,128)(2,1)S(1)}, u32[]{:S(2)}, u32[]{:S(2)}) %all-to-all-start.6) | async-done | bytes 1048608 | tf_op jit(solution)/shard_map/all_to_all | solution.py:444
  33.8 71.2 %conditional.1 = (f32[16,512]{1,0:T(8,128)S(1)}) conditional(s32[]{:T(128)} %clamp.3, (bf16[1024,1024]{1,0:T(8,128)(2,1)}, s32[32]{0:T(128)S(1)}, bf16[2048,2048]{1,0:T(8,128)(2,1)}, bf16[32,2,16,512]{3,2,1,0:T(8,128)(2,1)S(1)}, f32[2]{0:T(128)S(1)}) %tuple.24, (bf16[1024,1152]{1,0:T(8,128)(2,1)}, s32[32]{0:T(128)S(1)}, ...), branch_computations={%region_1.0_spmd, %region_3.0_spmd, %region_5.0_spmd} | conditional | flops 12148024320 | bytes 37814432 | solution.py:449
  33.8 5.1 %all-to-all-start.2 = ((bf16[32,2,16,1152]{3,2,1,0:T(8,128)(2,1)}), bf16[32,2,16,1152]{3,2,1,0:T(8,128)(2,1)S(1)}, u32[]{:S(2)}, u32[]{:S(2)}) async-start(bf16[32,2,16,1152]{3,2,1,0:T(8,128)(2,1)} %bitcast.12), calls=%async_computation.2 | async-start | bytes 4718592 | tf_op jit(solution)/shard_map/cond/branch_1_fun/all_to_all | solution.py:424
  38.9 16.1 %pack_green.4.green_ref = bf16[1664,1664]{1,0:T(8,128)(2,1)} custom-call(s32[32]{0:T(128)S(1)} %get-tuple-element.47.sizes_ref, bf16[2048,2048]{1,0:T(8,128)(2,1)} %get-tuple-element.48.green_ref), custom_call_target="tpu_custom_call" | custom-call | flops 10000000000 | bytes 14680064 | tf_op jit(solution)/shard_map/cond/branch_1_fun/pack_green/pallas_call | solution.py:302
  55.0 7.4 %dress.4.part_ref = f32[2,512,1792]{2,1,0:T(8,128)} custom-call(bf16[32,2,16,512]{3,2,1,0:T(8,128)(2,1)S(1)} %get-tuple-element.45.half_ref.half0_ref, bf16[1664,1664]{1,0:T(8,128)(2,1)} %pack_green.4.green_ref), custom_call_target="tpu_custom_call" | custom-call | flops 1744830464 | bytes 9568256 | tf_op jit(solution)/shard_map/cond/branch_1_fun/dress/pallas_call | solution.py:337
  62.4 7.6 %all-to-all-done.2.half1_ref = bf16[32,2,16,1152]{3,2,1,0:T(8,128)(2,1)S(1)} async-done(((bf16[32,2,16,1152]{3,2,1,0:T(8,128)(2,1)}), bf16[32,2,16,1152]{3,2,1,0:T(8,128)(2,1)S(1)}, u32[]{:S(2)}, u32[]{:S(2)}) %all-to-all-start.2) | async-done | bytes 2359328 | tf_op jit(solution)/shard_map/cond/branch_1_fun/all_to_all | solution.py:424
  70.1 10.9 %response.4 = bf16[512,512]{1,0:T(8,128)(2,1)S(1)} custom-call(f32[2]{0:T(128)S(1)} %get-tuple-element.44.weight_ref, bf16[32,2,16,512]{3,2,1,0:T(8,128)(2,1)S(1)} %get-tuple-element.45.half_ref.half0_ref, bf16[32,2,16,1152]{3,2,1,0:T(8,128)(2,1)S(1)} %all-to-all-done.2.half1_ref, bf16[1664,1664]{1,0:T(8,128)(2,1)} %pack_green.4.green_ref, ...), custom_call_target="tpu_custom_call" | custom-call | tf_op jit(solution)/shard_map/cond/branch_1_fun/response/pallas_call | solution.py:403
  81.0 15.3 %all_to_all.30 = bf16[32,16,512]{2,1,0:T(8,128)(2,1)S(1)} all-to-all(bf16[32,16,512]{2,1,0:T(8,128)(2,1)S(1)} %bitcast.9), channel_id=1, replica_groups=mesh['rep'=4,'ten'=32] {'ten'}, dimensions={0} | all-to-all | bytes 1048576 | tf_op jit(solution)/shard_map/cond/branch_1_fun/all_to_all | solution.py:429
  96.3 0.1 convert_reduce_fusion.1
  96.3 3.8 %collective-permute-start.5 = (f32[16,512]{1,0:T(8,128)S(1)}, f32[16,512]{1,0:T(8,128)S(1)}, u32[]{:S(2)}, u32[]{:S(2)}) collective-permute-start(f32[16,512]{1,0:T(8,128)S(1)} %convert_reduce_fusion.1), channel_id=1, source_target_pairs={{0,96},{32,0},{64,32},{96,64},{1,97},{33,1},{65,33},{97,65},{2,98}... | collective-permute-start | bytes 98312 | tf_op jit(solution)/shard_map/cond/branch_1_fun/ppermute | solution.py:433
  100.1 0.0 collective-permute-start.4
  100.1 1.3 %collective-permute-start.3 = (f32[16,512]{1,0:T(8,128)S(1)}, f32[16,512]{1,0:T(8,128)S(1)}, u32[]{:S(2)}, u32[]{:S(2)}) collective-permute-start(f32[16,512]{1,0:T(8,128)S(1)} %convert_reduce_fusion.1), channel_id=1, source_target_pairs={{0,64},{32,96},{64,0},{96,32},{1,65},{33,97},{65,1},{97,33},{2,66}... | collective-permute-start | bytes 98312 | tf_op jit(solution)/shard_map/cond/branch_1_fun/ppermute | solution.py:433
  101.4 0.0 collective-permute-done.5
  101.4 2.7 %collective-permute-done.4 = f32[16,512]{1,0:T(8,128)S(1)} collective-permute-done((f32[16,512]{1,0:T(8,128)S(1)}, f32[16,512]{1,0:T(8,128)S(1)}, u32[]{:S(2)}, u32[]{:S(2)}) %collective-permute-start.4) | collective-permute-done | bytes 32800 | tf_op jit(solution)/shard_map/cond/branch_1_fun/ppermute | solution.py:433
  104.1 0.4 collective-permute-done.3
  105.0 0.0 copy-start
  105.0 0.6 copy-done
  (1 shorter events, 0.0 us)
Async XLA Ops:
  0.0 16.9 %copy-start.2 = (s32[32]{0:T(128)S(1)}, s32[32]{0:T(128)}, u32[]{:S(2)}) copy-start(s32[32]{0:T(128)} %sizes_ref.3) | copy-start | bytes 388
  0.0 18.8 %copy-start.1 = (f32[64]{0:T(128)S(1)}, f32[64]{0:T(128)}, u32[]{:S(2)}) copy-start(f32[64]{0:T(128)} %param.13) | copy-start | bytes 772
  8.2 25.5 %all-to-all-start.6 = ((bf16[32,2,16,512]{3,2,1,0:T(8,128)(2,1)}), bf16[32,2,16,512]{3,2,1,0:T(8,128)(2,1)S(1)}, u32[]{:S(2)}, u32[]{:S(2)}) async-start(bf16[32,2,16,512]{3,2,1,0:T(8,128)(2,1)} %bitcast.14), calls=%async_computation.6 | async-start | bytes 2097152 | tf_op jit(solution)/shard_map/all_to_all | solution.py:444
  33.8 36.3 %all-to-all-start.2 = ((bf16[32,2,16,1152]{3,2,1,0:T(8,128)(2,1)}), bf16[32,2,16,1152]{3,2,1,0:T(8,128)(2,1)S(1)}, u32[]{:S(2)}, u32[]{:S(2)}) async-start(bf16[32,2,16,1152]{3,2,1,0:T(8,128)(2,1)} %bitcast.12), calls=%async_computation.2 | async-start | bytes 4718592 | tf_op jit(solution)/shard_map/cond/branch_1_fun/all_to_all | solution.py:424
  96.3 5.1 %collective-permute-start.5 = (f32[16,512]{1,0:T(8,128)S(1)}, f32[16,512]{1,0:T(8,128)S(1)}, u32[]{:S(2)}, u32[]{:S(2)}) collective-permute-start(f32[16,512]{1,0:T(8,128)S(1)} %convert_reduce_fusion.1), channel_id=1, source_target_pairs={{0,96},{32,0},{64,32},{96,64},{1,97},{33,1},{65,33},{97,65},{2,98}... | collective-permute-start | bytes 98312 | tf_op jit(solution)/shard_map/cond/branch_1_fun/ppermute | solution.py:433
  100.1 4.0 %collective-permute-start.4 = (f32[16,512]{1,0:T(8,128)S(1)}, f32[16,512]{1,0:T(8,128)S(1)}, u32[]{:S(2)}, u32[]{:S(2)}) collective-permute-start(f32[16,512]{1,0:T(8,128)S(1)} %convert_reduce_fusion.1), channel_id=1, source_target_pairs={{0,32},{32,64},{64,96},{96,0},{1,33},{33,65},{65,97},{97,1},{2,34}... | collective-permute-start | bytes 98312 | tf_op jit(solution)/shard_map/cond/branch_1_fun/ppermute | solution.py:433
  100.1 4.4 %collective-permute-start.3 = (f32[16,512]{1,0:T(8,128)S(1)}, f32[16,512]{1,0:T(8,128)S(1)}, u32[]{:S(2)}, u32[]{:S(2)}) collective-permute-start(f32[16,512]{1,0:T(8,128)S(1)} %convert_reduce_fusion.1), channel_id=1, source_target_pairs={{0,64},{32,96},{64,0},{96,32},{1,65},{33,97},{65,1},{97,33},{2,66}... | collective-permute-start | bytes 98312 | tf_op jit(solution)/shard_map/cond/branch_1_fun/ppermute | solution.py:433
  105.0 0.6 copy-start
